TPU v7x, 32 devices: a whole 2x2x4 slice. The times are simulated.
32 devices in a mesh: dp: 16 (over z, y, core), mp: 2 (over x).
Axes of the slice: x: 2, y: 2, z: 4, core: 2. Of those that a mesh axis runs over, the one named last changes fastest.
Arguments:
- images: bfloat16 [512, 14, 14, 384], P(('dp', 'mp')), may hold values from -6 to 6
- valid_slots: int32 [512], P(('dp', 'mp')), may hold values from 0 to 1, as said below
- keep_mask: int32 [512], P(('dp', 'mp')), may hold values 0 or 1
- dw_kernel: float32 [7, 7, 384], replicated, may hold values from -0.875 to 0.875
- dw_bias: float32 [384], replicated, may hold values from -3 to 3
- norm_gain: float32 [384], replicated, may hold values from 0.5 to 1.5
- norm_bias: float32 [384], replicated, may hold values from -2 to 2
- w_up: bfloat16 [384, 1536], P(None, 'mp'), may hold values from -0.3125 to 0.3125
- b_up: bfloat16 [1536], P('mp'), may hold values from -3 to 3
- w_down: bfloat16 [384, 1536], P(None, 'mp'), may hold values from -0.21875 to 0.21875
- b_down: float32 [384], replicated, may hold values from -2 to 2
- layer_scale: float32 [384], replicated, may hold values from 0.4 to 1.6
- ds_gain: float32 [384], replicated, may hold values from 0.5 to 1.5
- ds_bias: float32 [384], replicated, may hold values from -2 to 2
- ds_weight: bfloat16 [1536, 768], P(('dp', 'mp')), may hold values from -0.15625 to 0.15625
- ds_bias_out: float32 [768], replicated, may hold values from -2 to 2
- cotangent: bfloat16 [512, 7, 7, 768], P(('dp', 'mp')), may hold values from -6 to 6
Outputs:
- produced: bfloat16 [512, 7, 7, 768], P(('dp', 'mp'))
- grad_images: float32 [512, 14, 14, 384], P(('dp', 'mp'))
- grad_dw_kernel: float32 [7, 7, 384], replicated
- grad_dw_bias: float32 [384], replicated
- grad_norm_gain: float32 [384], replicated
- grad_norm_bias: float32 [384], replicated
- grad_w_up: float32 [384, 1536], P('dp', 'mp')
- grad_b_up: float32 [1536], replicated
- grad_w_down: float32 [384, 1536], P('dp', 'mp')
- grad_b_down: float32 [384], replicated
- grad_layer_scale: float32 [384], replicated
- grad_ds_gain: float32 [384], replicated
- grad_ds_bias: float32 [384], replicated
- grad_ds_weight: float32 [1536, 768], P(('dp', 'mp'))
- grad_ds_bias_out: float32 [768], replicated
Inputs may be any that keep to these rules, and one draw needn't show every extreme that they name: `valid_slots`: in each aligned group of 32 slots the valid ones come first; every group has 16 or more valid slots, one group exactly that many, and one group is all valid.
All inputs are finite; a program needn't handle non-finite values. No bound on the sum of `keep_mask` on one device may be relied on, other than what follows from the above.
Results may differ from a plain program's by a relative error of at most 0.0063.
Values may be sent and summed in bfloat16 or wider, within the bound.
No kernel may reach another device: no remote copies, remote signals or barrier semaphores. Data moves between devices by JAX's collectives and lax.ppermute only.
A program may use at most 512 MiB of HBM per device.

v0:
```python
import jax
import jax.numpy as jnp
from jax import lax
from jax.sharding import PartitionSpec as P

KERNEL = 7


KEEP_SCALE = 1.0 / 0.9


def depthwise(fields, kernel):
    reach = KERNEL // 2
    extent = fields.shape[1]
    padded = jnp.pad(fields, ((0, 0), (reach, reach), (reach, reach), (0, 0)))
    result = jnp.zeros_like(fields)
    for row_shift in range(KERNEL):
        for col_shift in range(KERNEL):
            result = (
                result
                + padded[:, row_shift : row_shift + extent, col_shift : col_shift + extent, :]
                * kernel[row_shift, col_shift]
            )
    return result


def layer_norm(values, gain, shift):
    center = values - jnp.mean(values, axis=-1, keepdims=True)
    spread = jnp.mean(center * center, axis=-1, keepdims=True)
    return center * lax.rsqrt(spread + 1e-06) * gain + shift


def norm_block(fields, kernel, conv_bias, gain, shift):
    return layer_norm(depthwise(fields, kernel) + conv_bias, gain, shift)


def exact_gelu(values):
    return jax.nn.gelu(values, approximate=False)


def to_patches(fields):
    number = fields.shape[0]
    half_side = fields.shape[1] // 2
    channels = fields.shape[3]
    arranged = fields.reshape(number, half_side, 2, half_side, 2, channels).transpose(
        0, 1, 3, 2, 4, 5
    )
    return arranged.reshape(number * half_side * half_side, 4 * channels)


def from_patches(values, number, half_side, channels):
    arranged = values.reshape(number, half_side, half_side, 2, 2, channels).transpose(
        0, 1, 3, 2, 4, 5
    )
    return arranged.reshape(number, 2 * half_side, 2 * half_side, channels)


def contract_last(left_mat, right_mat):
    return lax.dot_general(
        left_mat, right_mat, (((1,), (1,)), ((), ())), preferred_element_type=jnp.float32
    )


def contract_first(left_mat, right_mat):
    return lax.dot_general(
        left_mat, right_mat, (((0,), (0,)), ((), ())), preferred_element_type=jnp.float32
    )


def shards(
    images,
    valid_slots,
    keep_mask,
    dw_kernel,
    dw_bias,
    norm_gain,
    norm_bias,
    w_up,
    b_up,
    w_down,
    b_down,
    layer_scale,
    ds_gain,
    ds_bias,
    ds_weight,
    ds_bias_out,
    cotangent,
):
    images_dev = images.shape[0]
    channels = images.shape[3]
    half_side = images.shape[1] // 2
    fields = images.astype(jnp.float32)
    normed_f, norm_back = jax.vjp(norm_block, fields, dw_kernel, dw_bias, norm_gain, norm_bias)
    own_rows = normed_f.astype(jnp.bfloat16).reshape(-1, channels)
    keep_scale = keep_mask.astype(jnp.float32) * KEEP_SCALE
    hidden_dev = w_up.shape[1]
    hidden_all = hidden_dev * lax.axis_size("mp")
    group_rows = lax.all_gather(own_rows, "mp", axis=0, tiled=True)
    pre_act = jnp.dot(group_rows, w_up, preferred_element_type=jnp.float32) + b_up
    activated_f, gelu_back = jax.vjp(exact_gelu, pre_act)
    activated = activated_f.astype(jnp.bfloat16)
    branch_rows = (
        lax.psum_scatter(contract_last(activated, w_down), "mp", scatter_dimension=0, tiled=True)
        + b_down
    )
    branch = branch_rows.reshape(images.shape)
    per_image = keep_scale[:, None, None, None]
    block = fields + per_image * layer_scale * branch
    ds_normed_f, ds_back = jax.vjp(layer_norm, block, ds_gain, ds_bias)
    patches = to_patches(ds_normed_f.astype(jnp.bfloat16))
    out_channels = ds_weight.shape[1]
    ds_full = lax.all_gather(ds_weight, ("dp", "mp"), axis=0, tiled=True)
    projected = jnp.dot(patches, ds_full, preferred_element_type=jnp.float32)
    row_mask = jnp.repeat(valid_slots, half_side * half_side)[:, None]
    produced = ((projected + ds_bias_out) * row_mask.astype(jnp.float32)).astype(jnp.bfloat16)
    produced = produced.reshape(images_dev, half_side, half_side, out_channels)
    grad_out = cotangent.reshape(-1, out_channels) * row_mask.astype(jnp.bfloat16)
    grad_out_bias = jnp.sum(grad_out.astype(jnp.float32), axis=0)
    grad_ds_weight = lax.psum_scatter(
        contract_first(patches, grad_out), ("dp", "mp"), scatter_dimension=0, tiled=True
    )
    grad_patches = contract_last(grad_out, ds_full)
    grad_ds_normed = from_patches(grad_patches, images_dev, half_side, channels)
    grad_block, grad_ds_gain, grad_ds_bias = ds_back(grad_ds_normed)
    grad_scale = jnp.sum(grad_block * per_image * branch, axis=(0, 1, 2))
    grad_branch = (grad_block * per_image * layer_scale).astype(jnp.bfloat16).reshape(-1, channels)
    grad_b_down = jnp.sum(grad_branch.astype(jnp.float32), axis=0)
    grad_group = lax.all_gather(grad_branch, "mp", axis=0, tiled=True)
    grad_activated = jnp.dot(grad_group, w_down, preferred_element_type=jnp.float32)
    grad_pre = gelu_back(grad_activated)[0].astype(jnp.bfloat16)
    part_up = contract_first(group_rows, grad_pre)
    part_down = contract_first(grad_group, activated)
    grad_b_up = lax.dynamic_update_slice(
        jnp.zeros((hidden_all,), jnp.float32),
        jnp.sum(grad_pre.astype(jnp.float32), axis=0),
        (lax.axis_index("mp") * hidden_dev,),
    )
    grad_normed = lax.psum_scatter(
        contract_last(grad_pre, w_up), "mp", scatter_dimension=0, tiled=True
    )
    grad_w_up, grad_w_down = (
        lax.psum_scatter(part_up, "dp", scatter_dimension=0, tiled=True),
        lax.psum_scatter(part_down, "dp", scatter_dimension=0, tiled=True),
    )
    grad_fields, grad_kernel, grad_conv_bias, grad_gain, grad_shift = norm_back(
        grad_normed.reshape(images.shape)
    )
    summed = lax.psum(
        (
            grad_kernel,
            grad_conv_bias,
            grad_gain,
            grad_shift,
            grad_b_up,
            grad_b_down,
            grad_scale,
            grad_ds_gain,
            grad_ds_bias,
            grad_out_bias,
        ),
        ("dp", "mp"),
    )
    return (
        produced,
        grad_block + grad_fields,
        summed[0],
        summed[1],
        summed[2],
        summed[3],
        grad_w_up,
        summed[4],
        grad_w_down,
        summed[5],
        summed[6],
        summed[7],
        summed[8],
        grad_ds_weight,
        summed[9],
    )


def solution(mesh):
    in_specs = (
        P(("dp", "mp"), None, None, None),
        P(("dp", "mp")),
        P(("dp", "mp")),
        P(),
        P(),
        P(),
        P(),
        P(None, "mp"),
        P("mp"),
        P(None, "mp"),
        P(),
        P(),
        P(),
        P(),
        P(("dp", "mp"), None),
        P(),
        P(("dp", "mp"), None, None, None),
    )
    out_specs = (
        P(("dp", "mp"), None, None, None),
        P(("dp", "mp"), None, None, None),
        P(),
        P(),
        P(),
        P(),
        P("dp", "mp"),
        P(),
        P("dp", "mp"),
        P(),
        P(),
        P(),
        P(),
        P(("dp", "mp"), None),
        P(),
    )
    return jax.shard_map(shards, mesh=mesh, in_specs=in_specs, out_specs=out_specs, check_vma=False)
```

profile of v0, /device:TPU:0, one launch (start us, length us, event | category | flops | bytes accessed | tf_op | source)
XLA Modules:
  0.0 1040.9 jit_solution(13317017467616922073)
XLA Ops:
  11.8 4.6 copy_convert_fusion
  16.4 154.3 %fusion.17 = (f32[16,14,14]{2,1,0:T(8,128)S(1)}, f32[16,14,14,384]{3,2,1,0:T(8,128)S(1)}) fusion(f32[384]{0:T(512)S(1)} %copy-done.107, f32[384]{0:T(512)S(1)} %get-tuple-element.173, f32[384]{0:T(512)S(1)} %get-tuple-element.174, f32[384]{0:T(512)S(1)} %get-tuple-element.127, f32[384]{0:T(512)S(1)} %get-tuple-element.128, f32[384]{0:T(512)S(1)} %get-tuple-element.129, ...), kind=kLoop, calls=%fused_computation.263 | loop fusion | flops 119215040 | bytes 9723136 | tf_op jit(solution)/shard_map/jvp()/reduce_sum | solution.py:28
  176.4 4.9 reshape.437
  182.6 65.4 %all-gather.4.cloned.1.call-done = bf16[6272,384]{1,0:T(8,128)(2,1)} async-done(((bf16[3136,384]{1,0:T(8,128)(2,1)}), bf16[6272,384]{1,0:T(8,128)(2,1)}) %all-gather.4.cloned.1.call-update) | async-done | bytes 4816912 | tf_op jit(solution)/shard_map/all_gather | solution.py:98
  248.0 46.8 %multiply_convert_fusion = (bf16[6272,768]{1,0:T(8,128)(2,1)S(1)}, f32[6272,768]{1,0:T(8,128)}, f32[6272,768]{1,0:T(8,128)}) fusion(f32[768]{0:T(1024)S(1)} %convert_element_type.65, bf16[6272,384]{1,0:T(8,128)(2,1)} %all-gather.4.cloned.1.call-done, bf16[384,768]{1,0:T(8,128)(2,1)S(1)} %copy-done), kind=kOutput, calls=%fused_computation.52 | convolution fusion | flops 4017291264 | bytes 53578752 | tf_op jit(solution)/shard_map/dot_general | solution.py:99
  298.5 7.8 fusion.20
  308.7 4.9 fusion.19
  316.4 105.8 %reduce-scatter.6.cloned.1.call-done = f32[3136,384]{1,0:T(8,128)} async-done(((f32[6272,384]{1,0:T(8,128)}), f32[3136,384]{1,0:T(8,128)}) %reduce-scatter.6.cloned.1.call-update) | async-done | bytes 4816912 | tf_op jit(solution)/shard_map/reduce_scatter | solution.py:103
  422.2 4.8 broadcast_add_fusion.1
  427.0 6.2 reshape.438
  433.3 4.7 fusion.15
  443.4 4.4 fusion.14
  452.7 63.7 %all-gather.8.cloned.1.call-done = bf16[6272,384]{1,0:T(8,128)(2,1)} async-done(((bf16[3136,384]{1,0:T(8,128)(2,1)}), bf16[6272,384]{1,0:T(8,128)(2,1)}) %all-gather.8.cloned.1.call-update) | async-done | bytes 4816912 | tf_op jit(solution)/shard_map/all_gather | solution.py:128
  516.4 17.8 %convert_reduce_fusion = (f32[768]{0:T(1024)S(1)}, bf16[6272,768]{1,0:T(8,128)(2,1)S(1)}) fusion(f32[6272,768]{1,0:T(8,128)} %get-tuple-element.194, bf16[6272,384]{1,0:T(8,128)(2,1)} %all-gather.8.cloned.1.call-done, bf16[384,768]{1,0:T(8,128)(2,1)} %param.26, f32[6272,768]{1,0:T(8,128)} %get-tuple-element.250, f32[768]{0:T(1024)S(1)} %convert_element_type.65), kind=kOutput, calls=%fused_computation.50 | convolution fusion | flops 3781262592 | bytes 53581824 | tf_op jit(solution)/shard_map/dot_general | solution.py:129
  537.9 7.6 fusion.21
  557.3 6.9 fusion.24
  564.3 10.7 %fusion.22 = f32[384,768]{1,0:T(8,128)} fusion(bf16[6272,384]{1,0:T(8,128)(2,1)} %all-gather.4.cloned.1.call-done, bf16[6272,768]{1,0:T(8,128)(2,1)} %copy-done.6), kind=kOutput, calls=%fused_computation.268 | convolution fusion | flops 3699376128 | bytes 15630336 | tf_op jit(solution)/shard_map/dot_general | solution.py:65
  575.7 4.7 multiply_convert_fusion.2
  583.9 10.6 %fusion.23 = f32[384,768]{1,0:T(8,128)} fusion(bf16[6272,384]{1,0:T(8,128)(2,1)} %all-gather.8.cloned.1.call-done, bf16[6272,768]{1,0:T(8,128)(2,1)} %copy-done.5), kind=kOutput, calls=%fused_computation.269 | convolution fusion | flops 3699376128 | bytes 15630336 | tf_op jit(solution)/shard_map/dot_general | solution.py:65
  594.9 63.5 %reduce-scatter.8.cloned.1.call-done = f32[3136,384]{1,0:T(8,128)} async-done(((f32[6272,384]{1,0:T(8,128)}), f32[3136,384]{1,0:T(8,128)}) %reduce-scatter.8.cloned.1.call-update) | async-done | bytes 4816912 | tf_op jit(solution)/shard_map/reduce_scatter | solution.py:138
  658.4 6.3 reshape.444
  664.8 5.2 multiply_reduce_fusion.51
  675.4 35.9 %fusion.13 = (f32[384]{0:T(512)}, f32[384]{0:T(512)S(1)}, f32[384]{0:T(512)S(1)}, f32[384]{0:T(512)S(1)}, f32[384]{0:T(512)S(1)}, /*index=5*/f32[384]{0:T(512)S(...) fusion(bf16[16,14,14,384]{3,0,2,1:T(8,128)(2,1)} %param.17, ...), kind=kLoop, calls=%fused_computation.260 | loop fusion | flops 42142464 | bytes 21749248 | tf_op jit(solution)/shard_map/transpose(jvp())/reduce_sum | solution.py:34
  711.3 41.5 %multiply_reduce_fusion.49 = (f32[384]{0:T(512)S(1)}, f32[384]{0:T(512)S(1)}, f32[384]{0:T(512)S(1)}, f32[384]{0:T(512)S(1)}, f32[384]{0:T(512)S(1)}, /*index=5*...) fusion(f32[16,14,14,384]{3,2,1,0:T(8,128)} %get-tuple-element.1, ...), kind=kLoop, calls=%fused_computation.129 | loop fusion | flops 43345152 | bytes 9661440 | tf_op jit(solution)/shard_map/transpose(jvp())/reduce_sum | solution.py:21
  752.9 39.4 %multiply_reduce_fusion.50 = (f32[384]{0:T(512)S(1)}, f32[384]{0:T(512)S(1)}, f32[384]{0:T(512)S(1)}, f32[384]{0:T(512)S(1)}, f32[384]{0:T(512)S(1)}, /*index=5*...) fusion(f32[16,14,14,384]{3,2,1,0:T(8,128)} %get-tuple-element.1, ...), kind=kLoop, calls=%fused_computation.130 | loop fusion | flops 43345152 | bytes 9661440 | tf_op jit(solution)/shard_map/transpose(jvp())/reduce_sum | solution.py:21
  792.5 33.2 %broadcast_multiply_fusion.1 = (f32[16,14,14,384]{3,2,1,0:T(8,128)}, f32[16,14,14,384]{3,2,1,0:T(8,128)}, f32[16,14,14,384]{3,2,1,0:T(8,128)}, f32[16,14,14,384]...) fusion(f32[16,14,14,384]{3,2,1,0:T(8,128)} %get-tuple-element.1, ...), kind=kLoop, calls=%fused_computation.143 | loop fusion | flops 21676032 | bytes 91548672 | tf_op jit(solution)/shard_map/transpose(jvp())/mul | solution.py:21
  826.0 33.3 %broadcast_multiply_fusion = (f32[16,14,14,384]{3,2,1,0:T(8,128)}, f32[16,14,14,384]{3,2,1,0:T(8,128)}, f32[16,14,14,384]{3,2,1,0:T(8,128)}, f32[16,14,14,384]{3...) fusion(f32[16,14,14,384]{3,2,1,0:T(8,128)} %get-tuple-element.1, ...), kind=kLoop, calls=%fused_computation.142 | loop fusion | flops 21676032 | bytes 91548672 | tf_op jit(solution)/shard_map/transpose(jvp())/mul | solution.py:21
  860.8 24.6 %broadcast_multiply_fusion.2 = (f32[16,14,14,384]{3,2,1,0:T(8,128)}, f32[16,14,14,384]{3,2,1,0:T(8,128)}, f32[16,14,14,384]{3,2,1,0:T(8,128)}, f32[16,14,14,384]...) fusion(f32[16,14,14,384]{3,2,1,0:T(8,128)} %get-tuple-element.1, ...), kind=kLoop, calls=%fused_computation.144 | loop fusion | flops 15654912 | bytes 67456512 | tf_op jit(solution)/shard_map/transpose(jvp())/mul | solution.py:21
  885.5 80.8 %pad_add_fusion = f32[16,20,20,384]{3,2,1,0:T(8,128)} fusion(f32[16,14,14,384]{3,2,1,0:T(8,128)} %get-tuple-element.206, f32[16,14,14,384]{3,2,1,0:T(8,128)} %get-tuple-element.207, f32[16,14,14,384]{3,2,1,0:T(8,128)} %get-tuple-element.208, f32[16,14,14,384]{3,2,1,0:T(8,128)} %get-tuple-element.209, f32[16,14,14,384]{3,2,1,0:T(8,128)} %get-tuple-element.210, ...), kind=kLoop, calls=%fused_computation.66 | loop fusion | flops 103219200 | bytes 216956928 | tf_op jit(solution)/shard_map/transpose(jvp())/add_any | solution.py:21
  966.4 15.5 %fusion.7 = f32[16,14,14,384]{3,2,1,0:T(8,128)} fusion(f32[16,14,14,384]{3,2,1,0:T(8,128)} %get-tuple-element.200, f32[16,14,14,384]{3,2,1,0:T(8,128)} %get-tuple-element.201, f32[16,14,14,384]{3,2,1,0:T(8,128)} %get-tuple-element.202, f32[16,14,14,384]{3,2,1,0:T(8,128)} %get-tuple-element.203, f32[16,14,14,384]{3,2,1,0:T(8,128)} %get-tuple-element.204, ...), kind=kLoop, calls=%fused_computation.73 | loop fusion | flops 9633792 | bytes 43364608 | tf_op jit(solution)/shard_map/add | solution.py:165
  982.0 7.6 copy.53
  992.5 40.1 %all-reduce.99 = (f32[384]{0:T(512)}, f32[384]{0:T(512)}, f32[384]{0:T(512)}, f32[1536]{0:T(1024)}, f32[384]{0:T(512)}, /*index=5*/f32[384]{0:T(512)}, f32[384]{0:T(512)}, f32[384]{0:T(512)}, f32[768]{0:T(1024)}) all-reduce(f32[384]{0:T(512)S(1)} %copy-done.101, ...), channel_id=1, replica_groups=mesh['dp'=16,'mp'=2] {'dp','mp'}, use_global_device_ids=true, to_apply=%region_61.62 | all-reduce | flops 4992 | bytes 39936 | tf_op jit(solution)/shard_map/psum | solution.py:148
  (364 shorter events, 60.9 us)
Async XLA Ops:
  7.2 240.8 %copy-start = (bf16[384,768]{1,0:T(8,128)(2,1)S(1)}, bf16[384,768]{1,0:T(8,128)(2,1)}, u32[]{:S(2)}) copy-start(bf16[384,768]{1,0:T(8,128)(2,1)} %param.24) | copy-start | bytes 1769476
  7.2 240.8 %all-gather.4.cloned.1.call-start = ((), (), s32[]{:S(2)}) async-start(), calls=%async_computation.5 | async-start | bytes 7225344 | tf_op jit(solution)/shard_map/all_gather | solution.py:98
  8.2 162.5 %copy-start.49 = (f32[384]{0:T(512)}, f32[384]{0:T(512)S(1)}, u32[]{:S(2)}) copy-start(f32[384]{0:T(512)S(1)} %get-tuple-element.164) | copy-start | bytes 4612
  8.2 162.5 %copy-start.51 = (f32[384]{0:T(512)}, f32[384]{0:T(512)S(1)}, u32[]{:S(2)}) copy-start(f32[384]{0:T(512)S(1)} %get-tuple-element.165) | copy-start | bytes 4612
  8.2 162.5 %copy-start.53 = (f32[384]{0:T(512)}, f32[384]{0:T(512)S(1)}, u32[]{:S(2)}) copy-start(f32[384]{0:T(512)S(1)} %get-tuple-element.166) | copy-start | bytes 4612
  8.3 162.5 %copy-start.55 = (f32[384]{0:T(512)}, f32[384]{0:T(512)S(1)}, u32[]{:S(2)}) copy-start(f32[384]{0:T(512)S(1)} %get-tuple-element.167) | copy-start | bytes 4612
  8.3 162.5 %copy-start.57 = (f32[384]{0:T(512)}, f32[384]{0:T(512)S(1)}, u32[]{:S(2)}) copy-start(f32[384]{0:T(512)S(1)} %get-tuple-element.168) | copy-start | bytes 4612
  8.3 162.5 %copy-start.59 = (f32[384]{0:T(512)}, f32[384]{0:T(512)S(1)}, u32[]{:S(2)}) copy-start(f32[384]{0:T(512)S(1)} %get-tuple-element.169) | copy-start | bytes 4612
  8.3 162.5 %copy-start.61 = (f32[384]{0:T(512)}, f32[384]{0:T(512)S(1)}, u32[]{:S(2)}) copy-start(f32[384]{0:T(512)S(1)} %get-tuple-element.170) | copy-start | bytes 4612
  8.3 162.5 %copy-start.63 = (f32[384]{0:T(512)}, f32[384]{0:T(512)S(1)}, u32[]{:S(2)}) copy-start(f32[384]{0:T(512)S(1)} %get-tuple-element.171) | copy-start | bytes 4612
  8.3 162.5 %copy-start.65 = (f32[384]{0:T(512)}, f32[384]{0:T(512)S(1)}, u32[]{:S(2)}) copy-start(f32[384]{0:T(512)S(1)} %get-tuple-element.172) | copy-start | bytes 4612
  8.3 162.5 %copy-start.67 = (f32[384]{0:T(512)}, f32[384]{0:T(512)S(1)}, u32[]{:S(2)}) copy-start(f32[384]{0:T(512)S(1)} %get-tuple-element.173) | copy-start | bytes 4612
  8.3 162.5 %copy-start.85 = (f32[384]{0:T(512)}, f32[384]{0:T(512)S(1)}, u32[]{:S(2)}) copy-start(f32[384]{0:T(512)S(1)} %get-tuple-element.174) | copy-start | bytes 4612
  9.7 161.1 %copy-start.23 = (f32[384]{0:T(512)}, f32[384]{0:T(512)S(1)}, u32[]{:S(2)}) copy-start(f32[384]{0:T(512)S(1)} %get-tuple-element.127) | copy-start | bytes 4612
  9.7 161.1 %copy-start.25 = (f32[384]{0:T(512)}, f32[384]{0:T(512)S(1)}, u32[]{:S(2)}) copy-start(f32[384]{0:T(512)S(1)} %get-tuple-element.128) | copy-start | bytes 4612
  9.7 161.1 %copy-start.27 = (f32[384]{0:T(512)}, f32[384]{0:T(512)S(1)}, u32[]{:S(2)}) copy-start(f32[384]{0:T(512)S(1)} %get-tuple-element.129) | copy-start | bytes 4612
  9.7 161.1 %copy-start.29 = (f32[384]{0:T(512)}, f32[384]{0:T(512)S(1)}, u32[]{:S(2)}) copy-start(f32[384]{0:T(512)S(1)} %get-tuple-element.130) | copy-start | bytes 4612
  9.7 161.1 %copy-start.31 = (f32[384]{0:T(512)}, f32[384]{0:T(512)S(1)}, u32[]{:S(2)}) copy-start(f32[384]{0:T(512)S(1)} %get-tuple-element.131) | copy-start | bytes 4612
  9.7 161.1 %copy-start.33 = (f32[384]{0:T(512)}, f32[384]{0:T(512)S(1)}, u32[]{:S(2)}) copy-start(f32[384]{0:T(512)S(1)} %get-tuple-element.132) | copy-start | bytes 4612
  9.7 161.1 %copy-start.35 = (f32[384]{0:T(512)}, f32[384]{0:T(512)S(1)}, u32[]{:S(2)}) copy-start(f32[384]{0:T(512)S(1)} %get-tuple-element.133) | copy-start | bytes 4612
  9.7 161.1 %copy-start.37 = (f32[384]{0:T(512)}, f32[384]{0:T(512)S(1)}, u32[]{:S(2)}) copy-start(f32[384]{0:T(512)S(1)} %get-tuple-element.134) | copy-start | bytes 4612
  9.7 161.1 %copy-start.39 = (f32[384]{0:T(512)}, f32[384]{0:T(512)S(1)}, u32[]{:S(2)}) copy-start(f32[384]{0:T(512)S(1)} %get-tuple-element.135) | copy-start | bytes 4612
  9.7 161.1 %copy-start.41 = (f32[384]{0:T(512)}, f32[384]{0:T(512)S(1)}, u32[]{:S(2)}) copy-start(f32[384]{0:T(512)S(1)} %get-tuple-element.136) | copy-start | bytes 4612
  9.8 161.1 %copy-start.43 = (f32[384]{0:T(512)}, f32[384]{0:T(512)S(1)}, u32[]{:S(2)}) copy-start(f32[384]{0:T(512)S(1)} %get-tuple-element.137) | copy-start | bytes 4612
  181.4 127.3 %all-gather.6.cloned.1.call-start = ((), (), s32[]{:S(2)}) async-start(), calls=%async_computation.7 | async-start | bytes 2433024 | tf_op jit(solution)/shard_map/all_gather | solution.py:112
  182.1 240.1 %reduce-scatter.6.cloned.1.call-start = ((), (), s32[]{:S(2)}) async-start(), calls=%async_computation.6 | async-start | bytes 14450688 | tf_op jit(solution)/shard_map/reduce_scatter | solution.py:103
  306.4 210.0 %all-gather.8.cloned.1.call-start = ((), (), s32[]{:S(2)}) async-start(), calls=%async_computation.8 | async-start | bytes 7225344 | tf_op jit(solution)/shard_map/all_gather | solution.py:128
  452.5 205.9 %reduce-scatter.8.cloned.1.call-start = ((), (), s32[]{:S(2)}) async-start(), calls=%async_computation.9 | async-start | bytes 14450688 | tf_op jit(solution)/shard_map/reduce_scatter | solution.py:138
  545.6 487.1 %reduce-scatter.14.cloned.1.call-start = ((), (), s32[]{:S(2)}) async-start(), calls=%async_computation.13 | async-start | bytes 4866048 | tf_op jit(solution)/shard_map/reduce_scatter | solution.py:119
  564.2 468.4 %reduce-scatter.10.cloned.1.call-start = ((), (), s32[]{:S(2)}) async-start(), calls=%async_computation.11 | async-start | bytes 1253376 | tf_op jit(solution)/shard_map/reduce_scatter | solution.py:142
  575.0 457.7 %reduce-scatter.12.cloned.1.call-start = ((), (), s32[]{:S(2)}) async-start(), calls=%async_computation.12 | async-start | bytes 1253376 | tf_op jit(solution)/shard_map/reduce_scatter | solution.py:143
  594.5 438.1 %all-reduce.102.cloned.1.call-start = ((), (), s32[]{:S(2)}) async-start(), calls=%async_computation.10 | async-start | bytes 172032 | tf_op jit(solution)/shard_map/psum | solution.py:148
  (102 other events, 4891.4 us)
Sparse Core Ops, SparseCore 0:
  181.5 66.4 all-gather.3
  250.9 57.3 all-gather.5
  310.7 111.5 reduce-scatter.5
  452.6 63.7 all-gather.7
  545.7 112.6 reduce-scatter.7
  664.3 106.9 reduce-scatter.13
  775.9 57.0 reduce-scatter.9
  837.7 57.0 reduce-scatter.11
  901.9 118.5 all-reduce.101
where the time goes:
time: 1050 us; the launch traced here: 1040 us
  other arithmetic  502 us (48%)
  waiting for transfers between devices  299 us (28%)
  matrix products  118 us (11%)
  local copies, waits for them, and re-layouts  63.5 us (6%)
  blocking collectives  40.1 us (4%)
  between operations  16.3 us (2%)
    reduce_sum x3, other arithmetic, layer_norm(): center = values - jnp.mean(values, axis=-1, keepdims=True)  163 us
    reduce_scatter x1, waiting for transfers between devices, shards(): lax.psum_scatter(contract_last(activated, w_down), 'mp', scatter_dimensio...  106 us
    mul x3, other arithmetic, depthwise(): padded[:, row_shift:row_shift + extent, col_shift:col_shift + extent, :]  91.1 us
    reduce_sum x2, other arithmetic, depthwise(): padded[:, row_shift:row_shift + extent, col_shift:col_shift + extent, :]  80.9 us
    add_any x1, other arithmetic, depthwise(): padded[:, row_shift:row_shift + extent, col_shift:col_shift + extent, :]  80.8 us
    all_gather x1, waiting for transfers between devices, shards(): group_rows = lax.all_gather(own_rows, 'mp', axis=0, tiled=True)  65.4 us
    all_gather x1, waiting for transfers between devices, shards(): grad_group = lax.all_gather(grad_branch, 'mp', axis=0, tiled=True)  63.7 us
    reduce_scatter x1, waiting for transfers between devices, shards(): lax.psum_scatter(contract_last(grad_pre, w_up), 'mp', scatter_dimension=0...  63.5 us
  transfers between devices with their start and end apart: 9, of which 4 were waited for; matrix products, arithmetic and copies ran while one was open for 43% of the time, Pallas kernels for 0%

commit v1 on v0

v1 whole, which is shorter than its diff:
```python
import functools
import jax
import jax.numpy as jnp
import numpy as np
from jax import lax
from jax.experimental import pallas as pl
from jax.experimental.pallas import tpu as pltpu
from jax.sharding import PartitionSpec as P

KERNEL = 7
REACH = 3
KEEP_SCALE = 1.0 / 0.9
EPS = 1e-06
BF = jnp.bfloat16
F32 = jnp.float32
VMEM_LIMIT = 60 * 2**20


def split(values):
    high = values.astype(jnp.bfloat16)
    return high, (values - high.astype(np.float32)).astype(jnp.bfloat16)


@functools.cache
def tables(side):
    half, circle = side // 2, side + REACH
    wide = 8 * half
    pixels = 4 * wide
    spots = np.zeros((pixels, 2))
    real = np.zeros(pixels, bool)
    for a in range(2):
        for b in range(2):
            for i in range(half):
                for j in range(half):
                    p = (2 * a + b) * wide + 8 * i + j
                    spots[p] = 2 * i + a, 2 * j + b
                    real[p] = True
    waves = [(0, 0)]
    waves += [(u, 0) for u in range(1, circle // 2 + 1)]
    waves += [(u, v) for v in range(1, circle // 2 + 1) for u in range(circle)]
    waves = np.array(waves, float)
    count = len(waves)
    assert 2 * count - 1 == circle * circle
    tall = -(-count // 16) * 16 if count % 8 else count
    tall = -(-count // 8) * 8
    taps = np.array([(a - REACH, b - REACH) for a in range(KERNEL) for b in range(KERNEL)], float)
    turn = 2 * np.pi / circle

    def stack(points, keep, sine):
        angle = turn * waves @ points.T
        out = np.zeros((2 * tall, len(points)))
        out[:count] = np.cos(angle) * keep
        out[tall : tall + count] = sine * np.sin(angle) * keep
        return out

    weight = np.full(count, 2.0)
    weight[0] = 1.0
    weight = np.concatenate([np.pad(weight, (0, tall - count))] * 2) / circle**2
    ahead = stack(spots, real, -1.0)
    back = (stack(spots, real, -1.0) * weight[:, None]).T
    lift = stack(taps, np.ones(len(taps)), 1.0)
    drop = (stack(taps, np.ones(len(taps)), -1.0) * weight[:, None]).T
    tap_pad = -(-len(taps) // 8) * 8 - len(taps)
    lift = np.pad(lift, ((0, 0), (0, tap_pad)))
    drop = np.pad(drop, ((0, tap_pad), (0, 0)))
    ahead, back = ahead.astype(np.float32), back.astype(np.float32)
    ahead_hi, ahead_lo = split(ahead)
    back_hi, back_lo = split(back)
    return {
        "tall": tall,
        "wide": wide,
        "ahead2": np.concatenate([ahead_hi, ahead_lo], 1),
        "ahead3": np.concatenate([ahead_hi, ahead_lo, ahead_hi], 1),
        "back3": np.concatenate([back_hi, back_hi, back_lo], 1),
        "back2": np.concatenate([back_hi, back_lo], 1),
        "lift": lift.astype(np.float32),
        "drop": drop.astype(np.float32),
    }


def dot(left, right):
    return jnp.dot(left, right, preferred_element_type=F32)


def dot_nt(left, right):
    return lax.dot_general(left, right, (((1,), (1,)), ((), ())), preferred_element_type=F32)


def dot_tn(left, right):
    return lax.dot_general(left, right, (((0,), (0,)), ((), ())), preferred_element_type=F32)


def dot_f32(left, right):
    return lax.dot_general(
        left, right, (((1,), (0,)), ((), ())), precision=lax.Precision.HIGHEST, preferred_element_type=F32
    )


def fold(values):
    return jnp.sum(values.reshape(-1, 8, values.shape[-1]), axis=0)


def row_mean(values):
    return jnp.mean(values, axis=-1, keepdims=True)


def pair_order(first, second, wide):
    pieces = []
    for q in range(4):
        pieces += [first[q * wide : (q + 1) * wide], second[q * wide : (q + 1) * wide]]
    return jnp.concatenate(pieces, axis=0)


def image_of_pair(pair, n, wide):
    return jnp.concatenate([pair[(2 * q + n) * wide : (2 * q + n + 1) * wide] for q in range(4)], axis=0)


def conv_kernel(x_ref, k_ref, cb_ref, g_ref, s_ref, lift_ref, ahead_ref, back_ref,
                xp_ref, xh_ref, normed_ref, xhat_ref, rstd_ref, h_ref, nat):
    side = x_ref.shape[1]
    half = side // 2
    ch = x_ref.shape[3]
    wide = 8 * half
    tall = h_ref.shape[0] // 2

    @pl.when(pl.program_id(0) == 0)
    def _():
        h_ref[...] = dot_f32(lift_ref[...], k_ref[...])
        nat[...] = jnp.zeros_like(nat)

    images = x_ref.shape[0]
    patches = []
    for n in range(images):
        cols = []
        for c in range(ch // 128):
            nat[n, c, :, :side, :] = x_ref[n, :, :, c * 128 : (c + 1) * 128].astype(F32)
            rows = [nat[n, c, 2 * i + a, pl.ds(b, 8, stride=2), :] for a in range(2) for b in range(2) for i in range(half)]
            cols.append(jnp.concatenate(rows, axis=0))
        patches.append(jnp.concatenate(cols, axis=1))
    both = jnp.concatenate([p.astype(BF) for p in patches], axis=1)
    ahead = ahead_ref[...]
    spectrum = dot(ahead, jnp.concatenate([both, both], axis=0))
    h_re, h_im = h_ref[:tall], h_ref[tall:]
    highs, lows = [], []
    for n in range(images):
        cs = slice(n * ch, (n + 1) * ch)
        re, im = spectrum[:tall, cs], spectrum[tall:, cs]
        xh_ref[n] = spectrum[:, cs].astype(BF)
        out = jnp.concatenate([re * h_re - im * h_im, re * h_im + im * h_re], axis=0)
        high = out.astype(BF)
        highs.append(high)
        lows.append((out - high.astype(F32)).astype(BF))
    high, low = jnp.concatenate(highs, axis=1), jnp.concatenate(lows, axis=1)
    conv = dot(back_ref[...], jnp.concatenate([high, low, high], axis=0))
    pair = pair_order(conv[:, :ch], conv[:, ch:], wide) + cb_ref[...]
    center = pair - row_mean(pair)
    rstd = lax.rsqrt(row_mean(center * center) + EPS)
    xhat = center * rstd
    rstd_ref[...] = rstd
    xhat_ref[...] = xhat.astype(BF)
    normed_ref[...] = (xhat * g_ref[...] + s_ref[...]).astype(BF)
    xp_ref[...] = pair_order(patches[0], patches[1], wide).astype(BF)


def up_kernel(n_ref, w_ref, b_ref, act_ref, slope_ref, *, step):
    rows = n_ref[...]
    for lo in range(0, w_ref.shape[1], step):
        cs = slice(lo, lo + step)
        pre = dot(rows, w_ref[:, cs]) + b_ref[:, cs]
        scaled = pre * np.float32(np.sqrt(0.5))
        cdf = 0.5 * lax.erf(scaled) + 0.5
        bump = jnp.exp2(scaled * scaled * np.float32(-np.log2(np.e)))
        act_ref[:, cs] = (pre * cdf).astype(BF)
        slope_ref[:, cs] = (cdf + pre * np.float32(1 / np.sqrt(2 * np.pi)) * bump).astype(BF)


def ds_kernel(valid_ref, keep_ref, act_ref, xp_ref, cot_ref, wd_ref, bd_ref, sc_ref, dg_ref, db_ref, dsw_ref, dob_ref,
              prod_ref, gblock_ref, gbr_ref, gdsw_ref, sums_ref, obsum_ref, cpad, *, images):
    step = pl.program_id(0)
    ch = xp_ref.shape[1]
    half = cot_ref.shape[1]
    wide = 8 * half
    tile = images * 4 * wide

    @pl.when(step == 0)
    def _():
        cpad[...] = jnp.zeros_like(cpad)
        gdsw_ref[...] = jnp.zeros_like(gdsw_ref)
        sums_ref[...] = jnp.zeros_like(sums_ref)
        obsum_ref[...] = jnp.zeros_like(obsum_ref)

    branch = dot_nt(act_ref[...], wd_ref[...]) + bd_ref[...]
    scale = sc_ref[...]
    valid = [valid_ref[step * images + n].astype(F32) for n in range(images)]
    keep = [keep_ref[step * images + n].astype(F32) * np.float32(KEEP_SCALE) for n in range(images)]
    keep_scale = [k * scale for k in keep]

    def order(make):
        return [make(2 * p + n, ((p * 4 + q) * 2 + n) * wide) for p in range(images // 2) for q in range(4) for n in range(2)]

    kept = jnp.concatenate(order(lambda n, lo: branch[lo : lo + wide] * keep_scale[n]), axis=0)
    block = xp_ref[...].astype(F32) + kept
    center = block - row_mean(block)
    rstd = lax.rsqrt(row_mean(center * center) + EPS)
    xhat = center * rstd
    normed = (xhat * dg_ref[...] + db_ref[...]).astype(BF)

    def quarters(values):
        cols = []
        for q in range(4):
            cols.append(jnp.concatenate([values[(p * 4 + q) * 2 * wide : (p * 4 + q + 1) * 2 * wide] for p in range(images // 2)], axis=0))
        return cols

    patches = jnp.concatenate(quarters(normed), axis=1)
    projected = dot(patches, dsw_ref[...]) + dob_ref[...]
    for n in range(images):
        piece = projected[n * wide : (n + 1) * wide] * valid[n]
        prod_ref[n] = piece.reshape(half, 8, piece.shape[1])[:, :half].astype(BF)
        cpad[n, :, :half, :] = cot_ref[n].astype(F32) * valid[n]
    grad_out_f = cpad[...].reshape(images * wide, cpad.shape[3])
    obsum_ref[...] += fold(grad_out_f)
    grad_out = grad_out_f.astype(BF)
    gdsw_ref[...] += dot_tn(patches, grad_out)
    grad_patches = dot_nt(grad_out, dsw_ref[...])
    pieces = []
    for p in range(images // 2):
        for q in range(4):
            pieces.append(grad_patches[p * 2 * wide : (p + 1) * 2 * wide, q * ch : (q + 1) * ch])
    dy = jnp.concatenate(pieces, axis=0)
    dyx = dy * xhat
    sums_ref[0] += fold(dyx)
    sums_ref[1] += fold(dy)
    gain = dg_ref[...]
    dyg = dy * gain
    gblock = rstd * (dyg - row_mean(dyg) - xhat * row_mean(dyx * gain))
    gblock_ref[...] = gblock
    gkeep = jnp.concatenate(order(lambda n, lo: gblock[lo : lo + wide] * keep[n]), axis=0)
    sums_ref[2] += fold(gkeep * branch)
    gbr = (gkeep * scale).astype(BF)
    gbr_ref[...] = gbr
    sums_ref[3] += fold(gbr.astype(F32))


def mlp_kernel(gbr_ref, n_ref, act_ref, slope_ref, wd_ref, wu_ref, gn_ref, gwu_ref, gwd_ref, gbu_ref, *, step):
    @pl.when(pl.program_id(0) == 0)
    def _():
        gwu_ref[...] = jnp.zeros_like(gwu_ref)
        gwd_ref[...] = jnp.zeros_like(gwd_ref)
        gbu_ref[...] = jnp.zeros_like(gbu_ref)

    gbr = gbr_ref[...]
    gbr_t = gbr.T
    n_t = n_ref[...].T
    total = None
    for lo in range(0, wd_ref.shape[1], step):
        cs = slice(lo, lo + step)
        gact = dot(gbr, wd_ref[:, cs])
        gpre_f = gact * slope_ref[:, cs].astype(F32)
        gpre = gpre_f.astype(BF)
        gbu_ref[:, cs] += fold(gpre_f)
        gwu_ref[:, cs] += dot(n_t, gpre)
        gwd_ref[:, cs] += dot(gbr_t, act_ref[:, cs])
        part = dot_nt(gpre, wu_ref[:, cs])
        total = part if total is None else total + part
    gn_ref[...] = total


def back_kernel(gn_ref, xhat_ref, rstd_ref, gblock_ref, xh_ref, h_ref, g_ref, ahead_ref, back_ref, drop_ref,
                out_ref, dk_ref, sums_ref, acc, nat):
    images, side = out_ref.shape[0], out_ref.shape[1]
    half = side // 2
    wide = 8 * half
    ch = out_ref.shape[3]
    tall = h_ref.shape[0] // 2

    @pl.when(pl.program_id(0) == 0)
    def _():
        acc[...] = jnp.zeros_like(acc)
        sums_ref[...] = jnp.zeros_like(sums_ref)

    dy = gn_ref[...]
    xhat = xhat_ref[...].astype(F32)
    gain = g_ref[...]
    dyx = dy * xhat
    sums_ref[0] += fold(dyx)
    sums_ref[1] += fold(dy)
    dyg = dy * gain
    gconv = rstd_ref[...] * (dyg - row_mean(dyg) - xhat * row_mean(dyx * gain))
    sums_ref[2] += fold(gconv)
    high = gconv.astype(BF)
    low = (gconv - high.astype(F32))
    highs, lows = [], []
    for n in range(images):
        piece = image_of_pair(gconv, n, wide)
        h = piece.astype(BF)
        highs.append(h)
        lows.append((piece - h.astype(F32)).astype(BF))
    high, low = jnp.concatenate(highs, axis=1), jnp.concatenate(lows, axis=1)
    spectrum = dot(ahead_ref[...], jnp.concatenate([high, high, low], axis=0))
    h_re, h_im = h_ref[:tall], h_ref[tall:]
    highs, lows = [], []
    for n in range(images):
        cs = slice(n * ch, (n + 1) * ch)
        re, im = spectrum[:tall, cs], spectrum[tall:, cs]
        x_re, x_im = xh_ref[n, :tall].astype(F32), xh_ref[n, tall:].astype(F32)
        acc[:tall] += re * x_re + im * x_im
        acc[tall:] += re * x_im - im * x_re
        out = jnp.concatenate([re * h_re + im * h_im, im * h_re - re * h_im], axis=0)
        h = out.astype(BF)
        highs.append(h)
        lows.append((out - h.astype(F32)).astype(BF))
    high, low = jnp.concatenate(highs, axis=1), jnp.concatenate(lows, axis=1)
    grad = dot(back_ref[...], jnp.concatenate([high, low, high], axis=0))
    for n in range(images):
        piece = grad[:, n * ch : (n + 1) * ch] + image_of_pair(gblock_ref[...], n, wide)
        for a in range(2):
            for b in range(2):
                for i in range(half):
                    lo = (2 * a + b) * wide + 8 * i
                    for c in range(ch // 128):
                        nat[n, c, 2 * i + a, pl.ds(b, 8, stride=2), :] = piece[lo : lo + 8, c * 128 : (c + 1) * 128]
        for c in range(ch // 128):
            out_ref[n, :, :, c * 128 : (c + 1) * 128] = nat[n, c, :, :side, :]

    @pl.when(pl.program_id(0) == pl.num_programs(0) - 1)
    def _():
        dk_ref[...] = dot_f32(drop_ref[...], acc[...])


def params():
    return pltpu.CompilerParams(dimension_semantics=("arbitrary",), vmem_limit_bytes=VMEM_LIMIT)


def whole(array):
    return pl.BlockSpec(array.shape, lambda s, *_: (0,) * len(array.shape))


def whole_shape(shape):
    return pl.BlockSpec(shape, lambda s, *_: (0,) * len(shape))


def rows_spec(rows, cols):
    return pl.BlockSpec((rows, cols), lambda s, *_: (s, 0))


def lead_spec(shape):
    return pl.BlockSpec(shape, lambda s, *_: (s,) + (0,) * (len(shape) - 1))


def run_conv(images, kernel, conv_bias, gain, shift):
    number, side, _, ch = images.shape
    t = tables(side)
    tall, wide = t["tall"], t["wide"]
    rows = number * 4 * wide
    pair = 8 * wide
    taps = jnp.pad(kernel.reshape(KERNEL * KERNEL, ch), ((0, t["lift"].shape[1] - KERNEL * KERNEL), (0, 0)))
    args = (images, taps, conv_bias[None], gain[None], shift[None], jnp.asarray(t["lift"]), jnp.asarray(t["ahead2"]), jnp.asarray(t["back3"]))
    return pl.pallas_call(
        conv_kernel,
        grid=(number // 2,),
        in_specs=[lead_spec((2, side, side, ch))] + [whole(a) for a in args[1:]],
        out_shape=(
            jax.ShapeDtypeStruct((rows, ch), BF),
            jax.ShapeDtypeStruct((number, 2 * tall, ch), BF),
            jax.ShapeDtypeStruct((rows, ch), BF),
            jax.ShapeDtypeStruct((rows, ch), BF),
            jax.ShapeDtypeStruct((rows, 1), F32),
            jax.ShapeDtypeStruct((2 * tall, ch), F32),
        ),
        out_specs=(
            rows_spec(pair, ch),
            lead_spec((2, 2 * tall, ch)),
            rows_spec(pair, ch),
            rows_spec(pair, ch),
            rows_spec(pair, 1),
            whole_shape((2 * tall, ch)),
        ),
        scratch_shapes=[pltpu.VMEM((2, ch // 128, side, side + 2, 128), F32)],
        compiler_params=params(),
        name="conv_norm",
    )(*args)


def run_up(normed, w_up, b_up, tile, step):
    rows, ch = normed.shape
    hid = w_up.shape[1]
    return pl.pallas_call(
        functools.partial(up_kernel, step=step),
        grid=(rows // tile,),
        in_specs=[rows_spec(tile, ch), whole(w_up), whole_shape((1, hid))],
        out_shape=(jax.ShapeDtypeStruct((rows, hid), BF),) * 2,
        out_specs=(rows_spec(tile, hid),) * 2,
        compiler_params=params(),
        name="up_gelu",
    )(normed, w_up, b_up.astype(F32)[None])


def run_ds(valid, keep, act, xp, cot, w_down, b_down, scale, gain, shift, dsw, dob, images):
    rows, ch = xp.shape
    number, half, _, out_ch = cot.shape
    wide = 8 * half
    tile = images * 4 * wide
    args = (act, xp, cot, w_down, b_down[None], scale[None], gain[None], shift[None], dsw, dob[None])
    return pl.pallas_call(
        functools.partial(ds_kernel, images=images),
        grid_spec=pltpu.PrefetchScalarGridSpec(
            num_scalar_prefetch=2,
            grid=(number // images,),
            in_specs=[rows_spec(tile, act.shape[1]), rows_spec(tile, ch), lead_spec((images, half, half, out_ch))]
            + [whole(a) for a in args[3:]],
            out_specs=(
                lead_spec((images, half, half, out_ch)),
                rows_spec(tile, ch),
                rows_spec(tile, ch),
                whole_shape(dsw.shape),
                whole_shape((4, 8, ch)),
                whole_shape((8, out_ch)),
            ),
            scratch_shapes=[pltpu.VMEM((images, half, 8, out_ch), F32)],
        ),
        out_shape=(
            jax.ShapeDtypeStruct(cot.shape, BF),
            jax.ShapeDtypeStruct((rows, ch), F32),
            jax.ShapeDtypeStruct((rows, ch), BF),
            jax.ShapeDtypeStruct(dsw.shape, F32),
            jax.ShapeDtypeStruct((4, 8, ch), F32),
            jax.ShapeDtypeStruct((8, out_ch), F32),
        ),
        compiler_params=params(),
        name="downsample",
    )(valid, keep, *args)


def run_mlp(gbr, normed, act, slope, w_down, w_up, tile, step):
    rows, ch = gbr.shape
    hid = act.shape[1]
    return pl.pallas_call(
        functools.partial(mlp_kernel, step=step),
        grid=(rows // tile,),
        in_specs=[rows_spec(tile, ch), rows_spec(tile, ch), rows_spec(tile, hid), rows_spec(tile, hid), whole(w_down), whole(w_up)],
        out_shape=(
            jax.ShapeDtypeStruct((rows, ch), F32),
            jax.ShapeDtypeStruct((ch, hid), F32),
            jax.ShapeDtypeStruct((ch, hid), F32),
            jax.ShapeDtypeStruct((8, hid), F32),
        ),
        out_specs=(rows_spec(tile, ch), whole_shape((ch, hid)), whole_shape((ch, hid)), whole_shape((8, hid))),
        compiler_params=params(),
        name="mlp_back",
    )(gbr, normed, act, slope, w_down, w_up)


def run_back(gn, xhat, rstd, gblock, xh, h, gain, number, side):
    rows, ch = gn.shape
    t = tables(side)
    tall, wide = t["tall"], t["wide"]
    pair = 8 * wide
    drop = jnp.asarray(t["drop"])
    args = (gn, xhat, rstd, gblock, xh, h, gain[None], jnp.asarray(t["ahead3"]), jnp.asarray(t["back3"]), drop)
    return pl.pallas_call(
        back_kernel,
        grid=(number // 2,),
        in_specs=[rows_spec(pair, ch), rows_spec(pair, ch), rows_spec(pair, 1), rows_spec(pair, ch), lead_spec((2, 2 * tall, ch))]
        + [whole(a) for a in args[5:]],
        out_shape=(
            jax.ShapeDtypeStruct((number, side, side, ch), F32),
            jax.ShapeDtypeStruct((drop.shape[0], ch), F32),
            jax.ShapeDtypeStruct((3, 8, ch), F32),
        ),
        out_specs=(lead_spec((2, side, side, ch)), whole_shape((drop.shape[0], ch)), whole_shape((3, 8, ch))),
        scratch_shapes=[pltpu.VMEM((2 * tall, ch), F32), pltpu.VMEM((2, ch // 128, side, side + 2, 128), F32)],
        compiler_params=params(),
        name="conv_back",
    )(*args)


def local(images, valid, keep, dw_kernel, dw_bias, norm_gain, norm_bias, w_up, b_up, w_down, b_down,
          layer_scale, ds_gain, ds_bias, dsw, dob, cot):
    number, side = images.shape[:2]
    xp, xh, normed, xhat, rstd, h = run_conv(images, dw_kernel, dw_bias, norm_gain, norm_bias)
    act, slope = run_up(normed, w_up, b_up, 448, 512)
    produced, gblock, gbr, gdsw, sums, obsum = run_ds(valid, keep, act, xp, cot, w_down, b_down, layer_scale, ds_gain, ds_bias, dsw, dob, 4)
    gn, gwu, gwd, gbu = run_mlp(gbr, normed, act, slope, w_down, w_up, 896, 512)
    gimg, dk, sums2 = run_back(gn, xhat, rstd, gblock, xh, h, norm_gain, number, side)
    sums, sums2, gbu, obsum = sums.sum(1), sums2.sum(1), gbu.sum(0), obsum.sum(0)
    dk = dk[: KERNEL * KERNEL].reshape(dw_kernel.shape)
    return (produced, gimg, dk, sums2[2], sums2[0], sums2[1], gwu, gbu, gwd, sums[3], sums[2], sums[0], sums[1], gdsw, obsum)


def shards(images, valid_slots, keep_mask, dw_kernel, dw_bias, norm_gain, norm_bias, w_up, b_up, w_down, b_down,
           layer_scale, ds_gain, ds_bias, ds_weight, ds_bias_out, cotangent):
    w_up = lax.all_gather(w_up, "mp", axis=1, tiled=True)
    b_up = lax.all_gather(b_up, "mp", axis=0, tiled=True)
    w_down = lax.all_gather(w_down, "mp", axis=1, tiled=True)
    dsw = lax.all_gather(ds_weight, ("dp", "mp"), axis=0, tiled=True)
    out = local(images, valid_slots, keep_mask, dw_kernel, dw_bias, norm_gain, norm_bias, w_up, b_up, w_down, b_down,
                layer_scale, ds_gain, ds_bias, dsw, ds_bias_out, cotangent)
    produced, gimg, dk, dwb, ng, nb, gwu, gbu, gwd, gbd, gsc, dsg, dsb, gdsw, gob = out
    gdsw = lax.psum_scatter(gdsw, ("dp", "mp"), scatter_dimension=0, tiled=True)

    def spread(part):
        part = lax.psum_scatter(part, "mp", scatter_dimension=1, tiled=True)
        return lax.psum_scatter(part, "dp", scatter_dimension=0, tiled=True)

    gwu, gwd = spread(gwu), spread(gwd)
    dk, dwb, ng, nb, gbu, gbd, gsc, dsg, dsb, gob = lax.psum((dk, dwb, ng, nb, gbu, gbd, gsc, dsg, dsb, gob), ("dp", "mp"))
    return (produced, gimg, dk, dwb, ng, nb, gwu, gbu, gwd, gbd, gsc, dsg, dsb, gdsw, gob)

def solution(mesh):
    in_specs = (
        P(("dp", "mp"), None, None, None),
        P(("dp", "mp")),
        P(("dp", "mp")),
        P(),
        P(),
        P(),
        P(),
        P(None, "mp"),
        P("mp"),
        P(None, "mp"),
        P(),
        P(),
        P(),
        P(),
        P(("dp", "mp"), None),
        P(),
        P(("dp", "mp"), None, None, None),
    )
    out_specs = (
        P(("dp", "mp"), None, None, None),
        P(("dp", "mp"), None, None, None),
        P(),
        P(),
        P(),
        P(),
        P("dp", "mp"),
        P(),
        P("dp", "mp"),
        P(),
        P(),
        P(),
        P(),
        P(("dp", "mp"), None),
        P(),
    )
    return jax.shard_map(shards, mesh=mesh, in_specs=in_specs, out_specs=out_specs, check_vma=False)
```

time: 1050 us -> 614 us (0.58)
  other arithmetic: 502 us -> 0.68 us
  waiting for transfers between devices: 299 us -> 432 us
  matrix products: 118 us -> 0 us
  Pallas kernels: 0 us -> 98.3 us
  local copies, waits for them, and re-layouts: 63.5 us -> 22.5 us
    reduce_sum x14 -> x4, other arithmetic: 301 us -> 0.08 us  [the longest x1 0.03 us: local(): sums2.sum(1)]
    reduce_scatter x5, waiting for transfers between devices: 169 us -> 288 us  [the longest x2 124 us: spread(): return lax.psum_scatter(part, 'dp', scatter_dimension=0, tiled=True)]
    dot_general x9 -> x0, matrix products: 118 us -> none  [the longest x1 46.8 us: shards(): jnp.dot(group_rows, w_up, preferred_element_type=jnp.float32) + b_up]
    pallas_call x0 -> x5, Pallas kernels: none -> 98.3 us  [the longest x1 27.8 us: run_mlp(): pl.pallas_call(functools.partial(mlp_kernel, step=step), grid=(rows // ti...]
    mul x5 -> x0, other arithmetic: 91.2 us -> none  [the longest x3 91.1 us: depthwise(): padded[:, row_shift:row_shift + extent, col_shift:col_shift + extent, :]]
    add_any x2 -> x0, other arithmetic: 81.7 us -> none  [the longest x1 80.8 us: depthwise(): padded[:, row_shift:row_shift + extent, col_shift:col_shift + extent, :]]
    psum x1, waiting for transfers between devices: 0.01 us -> 75.7 us  [shards(): lax.psum((dk, dwb, ng, nb, gbu, gbd, gsc, dsg, dsb, gob), ('dp', 'mp'))]
    all_gather x3, waiting for transfers between devices: 129 us -> 65.1 us  [the longest x1 60.3 us: shards(): dsw = lax.all_gather(ds_weight, ('dp', 'mp'), axis=0, tiled=True)]
  transfers between devices with their start and end apart: 9 -> 9, of which waited for: 4 -> 8; matrix products, arithmetic and copies ran while one was open for 43% -> 4% of each run, Pallas kernels for 0% -> 8%
where the time goes in v1:
time: 614 us
  waiting for transfers between devices  432 us (70%)
  Pallas kernels  98.3 us (16%)
  blocking collectives  45.5 us (7%)
  local copies, waits for them, and re-layouts  22.5 us (4%)
  between operations  14.1 us (2%)
    reduce_scatter x2, waiting for transfers between devices, spread(): return lax.psum_scatter(part, 'dp', scatter_dimension=0, tiled=True)  124 us
    reduce_scatter x1, waiting for transfers between devices, shards(): gdsw = lax.psum_scatter(gdsw, ('dp', 'mp'), scatter_dimension=0, tiled=True)  115 us
    psum x1, waiting for transfers between devices, shards(): lax.psum((dk, dwb, ng, nb, gbu, gbd, gsc, dsg, dsb, gob), ('dp', 'mp'))  75.7 us
    all_gather x1, waiting for transfers between devices, shards(): dsw = lax.all_gather(ds_weight, ('dp', 'mp'), axis=0, tiled=True)  60.3 us
    reduce_scatter x2, waiting for transfers between devices, spread(): part = lax.psum_scatter(part, 'mp', scatter_dimension=1, tiled=True)  49.7 us
    psum x1, blocking collectives, shards(): lax.psum((dk, dwb, ng, nb, gbu, gbd, gsc, dsg, dsb, gob), ('dp', 'mp'))  40.3 us
    pallas_call x1, Pallas kernels, run_mlp(): pl.pallas_call(functools.partial(mlp_kernel, step=step), grid=(rows // ti...  27.8 us
    pallas_call x1, Pallas kernels, run_ds(): pl.pallas_call(functools.partial(ds_kernel, images=images), grid_spec=plt...  24 us
  transfers between devices with their start and end apart: 9, of which 8 were waited for; matrix products, arithmetic and copies ran while one was open for 4% of the time, Pallas kernels for 8%

profile of v1, /device:TPU:0, one launch (start us, length us, event | category | flops | bytes accessed | tf_op | source)
XLA Modules:
  0.0 613.8 jit_solution(9892900264211804492)
XLA Ops:
  7.2 0.7 all-gather.5.cloned.1.call-update
  8.0 0.7 all-gather.7.cloned.1.call-update
  8.8 0.7 all-gather.9.cloned.1.call-update
  9.6 3.8 copy.41.x_ref
  13.4 0.6 broadcast_in_dim.30.cb_ref
  14.0 0.6 broadcast_in_dim.31.g_ref
  14.5 0.6 broadcast_in_dim.32.s_ref
  15.1 5.2 all-gather
  20.3 0.6 convert.1.b_ref
  20.9 1.5 copy.42.cot_ref
  22.4 0.6 broadcast_in_dim.35.bd_ref
  24.7 0.6 broadcast_in_dim.39.dob_ref
  25.3 0.6 pad.4.k_ref
  25.9 13.0 %conv_norm.1 = (bf16[3584,384]{1,0:T(8,128)(2,1)}, bf16[16,304,384]{2,1,0:T(8,128)(2,1)}, bf16[3584,384]{1,0:T(8,128)(2,1)}, bf16[3584,384]{1,0:T(8,128)(2,1)}, f32[3584,1]{1,0:T(8,128)}, /*index=5*/f32[304,384]{1,0:T(8,128)}) custom-call(bf16[16,14,14,384]{3,2,1,0:T(8,128)(2,1)} %copy.41.x_ref, f32[56,384]{1,0:T(8,128)} %pad.4.k_ref, ...), custom_call_target="tpu_custom_call" | custom-call | tf_op jit(solution)/shard_map/conv_norm/pallas_call | solution.py:358
  38.9 15.8 %up_gelu.1 = (bf16[3584,1536]{1,0:T(8,128)(2,1)}, bf16[3584,1536]{1,0:T(8,128)(2,1)}) custom-call(bf16[3584,384]{1,0:T(8,128)(2,1)} %get-tuple-element.36.n_ref, bf16[384,1536]{1,0:T(8,128)(2,1)} %all-gather.5.cloned.1.call-done.w_ref.wu_ref, f32[1,1536]{1,0:T(1,128)} %convert.1.b_ref), custom_call_target="tpu_custom_call" | custom-call | tf_op jit(solution)/shard_map/up_gelu/pallas_call | solution.py:387
  54.7 4.7 all-gather.7.cloned.1.call-done.wd_ref
  59.4 60.3 %all-gather.9.cloned.1.call-done.dsw_ref = bf16[1536,768]{1,0:T(8,128)(2,1)} async-done(((bf16[48,768]{1,0:T(8,128)(2,1)}), bf16[1536,768]{1,0:T(8,128)(2,1)}) %all-gather.9.cloned.1.call-update) | async-done | bytes 2359312 | tf_op jit(solution)/shard_map/all_gather | solution.py:495
  119.8 24.0 %downsample.1 = (bf16[16,7,7,768]{3,2,1,0:T(8,128)(2,1)}, f32[3584,384]{1,0:T(8,128)}, bf16[3584,384]{1,0:T(8,128)(2,1)}, f32[1536,768]{1,0:T(8,128)}, f32[4,8,384]{2,1,0:T(8,128)}, /*index=5*/f32[8,768]{1,0:T(8,128)}) custom-call(s32[16]{0:T(128)} %valid_ref.1, s32[16]{0:T(128)} %keep_ref.1, bf16[3584,1536]{1,0:T(8,128)(2,1)} %get-tuple-element.37.act_ref, ...), custom_call_target="tpu_custom_call" | custom-call | tf_op jit(solution)/shard_map/downsample/pallas_call | solution.py:404
  143.7 27.8 %mlp_back.1 = (f32[3584,384]{1,0:T(8,128)}, f32[384,1536]{1,0:T(8,128)}, f32[384,1536]{1,0:T(8,128)}, f32[8,1536]{1,0:T(8,128)}) custom-call(bf16[3584,384]{1,0:T(8,128)(2,1)} %get-tuple-element.40.gbr_ref, bf16[3584,384]{1,0:T(8,128)(2,1)} %get-tuple-element.36.n_ref, bf16[3584,1536]{1,0:T(8,128)(2,1)} %get-tuple-element.37.act_ref, ...), custom_call_target="tpu_custom_call" | custom-call | tf_op jit(solution)/shard_map/mlp_back/pallas_call | solution.py:437
  172.3 17.8 %conv_back.1 = (f32[16,14,14,384]{3,2,1,0:T(8,128)}, f32[56,384]{1,0:T(8,128)}, f32[3,8,384]{2,1,0:T(8,128)}) custom-call(f32[3584,384]{1,0:T(8,128)} %get-tuple-element.42.gn_ref, bf16[3584,384]{1,0:T(8,128)(2,1)} %get-tuple-element.43.xhat_ref, f32[3584,1]{1,0:T(8,128)} %get-tuple-element.44.rstd_ref, f32[3584,384]{1,0:T(8,128)} %get-tuple-element.45.gblock_ref, ...), custom_call_target="tpu_custom_call" | custom-call | tf_op jit(solution)/shard_map/conv_back/pallas_call | solution.py:460
  190.1 1.5 reshape.37
  191.7 0.7 reduce-scatter.14.cloned.1.call-update
  192.5 12.8 %reduce-scatter.6.cloned.1.call-done = f32[384,768]{1,0:T(8,128)} async-done(((f32[384,1536]{1,0:T(8,128)}), f32[384,768]{1,0:T(8,128)}) %reduce-scatter.6.cloned.1.call-update) | async-done | bytes 1179664 | tf_op jit(solution)/shard_map/reduce_scatter | solution.py:502
  205.3 36.9 %reduce-scatter.10.cloned.1.call-done = f32[384,768]{1,0:T(8,128)} async-done(((f32[384,1536]{1,0:T(8,128)}), f32[384,768]{1,0:T(8,128)}) %reduce-scatter.10.cloned.1.call-update) | async-done | bytes 1179664 | tf_op jit(solution)/shard_map/reduce_scatter | solution.py:502
  242.2 1.3 copy.43
  243.5 7.6 %copy.44 = f32[16,14,14,384]{3,0,2,1:T(8,128)} copy(f32[16,14,14,384]{3,2,1,0:T(8,128)} %get-tuple-element.73) | data formatting | bytes 9633792
  251.3 40.3 %all-reduce.1 = (f32[384]{0:T(512)}, f32[384]{0:T(512)}, f32[384]{0:T(512)}, f32[1536]{0:T(1024)}, f32[384]{0:T(512)}, /*index=5*/f32[384]{0:T(512)}, f32[384]{0:T(512)}, f32[384]{0:T(512)}, f32[768]{0:T(1024)}) all-reduce(f32[384]{0:T(512)S(1)} %get-tuple-element.103, ...), channel_id=1, replica_groups=mesh['dp'=16,'mp'=2] {'dp','mp'}, use_global_device_ids=true, to_apply=%region_2.3 | all-reduce | flops 4992 | bytes 39936 | tf_op jit(solution)/shard_map/psum | solution.py:506
  291.5 75.7 %all-reduce.4.cloned.1.call-done = f32[7,7,384]{2,1,0:T(8,128)} async-done(((f32[7,7,384]{2,1,0:T(8,128)}), f32[7,7,384]{2,1,0:T(8,128)}) %all-reduce.4.cloned.1.call-update) | async-done | bytes 75280 | tf_op jit(solution)/shard_map/psum | solution.py:506
  367.2 115.0 %reduce-scatter.14.cloned.1.call-done = f32[48,768]{1,0:T(8,128)} async-done(((f32[1536,768]{1,0:T(8,128)}), f32[48,768]{1,0:T(8,128)}) %reduce-scatter.14.cloned.1.call-update) | async-done | bytes 147472 | tf_op jit(solution)/shard_map/reduce_scatter | solution.py:499
  482.2 61.8 %reduce-scatter.8.cloned.1.call-done = f32[24,768]{1,0:T(8,128)} async-done(((f32[384,768]{1,0:T(8,128)}), f32[24,768]{1,0:T(8,128)}) %reduce-scatter.8.cloned.1.call-update) | async-done | bytes 73744 | tf_op jit(solution)/shard_map/reduce_scatter | solution.py:503
  544.0 61.7 %reduce-scatter.12.cloned.1.call-done = f32[24,768]{1,0:T(8,128)} async-done(((f32[384,768]{1,0:T(8,128)}), f32[24,768]{1,0:T(8,128)}) %reduce-scatter.12.cloned.1.call-update) | async-done | bytes 73744 | tf_op jit(solution)/shard_map/reduce_scatter | solution.py:503
  605.7 1.5 copy.46
  (57 shorter events, 3.1 us)
Async XLA Ops:
  7.2 31.7 %all-gather.5.cloned.1.call-start = ((), (), s32[]{:S(2)}) async-start(), calls=%async_computation.5 | async-start | bytes 1769472 | tf_op jit(solution)/shard_map/all_gather | solution.py:492
  7.9 51.5 %all-gather.7.cloned.1.call-start = ((), (), s32[]{:S(2)}) async-start(), calls=%async_computation.6 | async-start | bytes 1769472 | tf_op jit(solution)/shard_map/all_gather | solution.py:494
  8.7 4.7 copy-start.2
  8.7 4.7 copy-start.8
  8.7 5.3 copy-start.9
  8.7 5.8 copy-start.10
  8.7 6.4 %copy-start.15 = (bf16[768]{0:T(1024)(128)(2,1)S(1)}, bf16[768]{0:T(1024)(128)(2,1)}, u32[]{:S(2)}) copy-start(bf16[768]{0:T(1024)(128)(2,1)} %param.30) | copy-start | bytes 4612
  8.7 12.2 %copy-start.1 = (bf16[16,7,7,768]{3,0,2,1:T(8,128)(2,1)S(1)}, bf16[16,7,7,768]{3,0,2,1:T(8,128)(2,1)}, u32[]{:S(2)}) copy-start(bf16[16,7,7,768]{3,0,2,1:T(8,128)(2,1)} %param.38) | copy-start | bytes 3612676
  8.7 111.0 %all-gather.9.cloned.1.call-start = ((), (), s32[]{:S(2)}) async-start(), calls=%async_computation.7 | async-start | bytes 2433024 | tf_op jit(solution)/shard_map/all_gather | solution.py:495
  9.5 12.9 %copy-start.11 = (f32[384]{0:T(512)S(1)}, f32[384]{0:T(512)}, u32[]{:S(2)}) copy-start(f32[384]{0:T(512)} %param.32) | copy-start | bytes 4612
  9.5 13.5 %copy-start.12 = (f32[384]{0:T(512)S(1)}, f32[384]{0:T(512)}, u32[]{:S(2)}) copy-start(f32[384]{0:T(512)} %param.33) | copy-start | bytes 4612
  9.5 14.1 %copy-start.13 = (f32[384]{0:T(512)S(1)}, f32[384]{0:T(512)}, u32[]{:S(2)}) copy-start(f32[384]{0:T(512)} %param.34) | copy-start | bytes 4612
  9.5 14.6 %copy-start.14 = (f32[384]{0:T(512)S(1)}, f32[384]{0:T(512)}, u32[]{:S(2)}) copy-start(f32[384]{0:T(512)} %param.35) | copy-start | bytes 4612
  9.5 15.2 %copy-start.7 = (f32[768]{0:T(1024)S(1)}, f32[768]{0:T(1024)}, u32[]{:S(2)}) copy-start(f32[768]{0:T(1024)} %param.37) | copy-start | bytes 9220
  9.5 195.8 %reduce-scatter.6.cloned.1.call-start = ((), (), s32[]{:S(2)}) async-start(), calls=%async_computation.9 | async-start | bytes 3538944 | tf_op jit(solution)/shard_map/reduce_scatter | solution.py:502
  171.5 70.7 %reduce-scatter.10.cloned.1.call-start = ((), (), s32[]{:S(2)}) async-start(), calls=%async_computation.11 | async-start | bytes 3538944 | tf_op jit(solution)/shard_map/reduce_scatter | solution.py:502
  172.1 195.1 %all-reduce.4.cloned.1.call-start = ((), (), s32[]{:S(2)}) async-start(), calls=%async_computation.8 | async-start | bytes 172032 | tf_op jit(solution)/shard_map/psum | solution.py:506
  191.7 290.5 %reduce-scatter.14.cloned.1.call-start = ((), (), s32[]{:S(2)}) async-start(), calls=%async_computation.13 | async-start | bytes 4866048 | tf_op jit(solution)/shard_map/reduce_scatter | solution.py:499
  191.7 50.5 %copy-start = (bf16[16,7,7,768]{3,2,1,0:T(8,128)(2,1)S(1)}, bf16[16,7,7,768]{3,2,1,0:T(8,128)(2,1)}, u32[]{:S(2)}) copy-start(bf16[16,7,7,768]{3,2,1,0:T(8,128)(2,1)} %get-tuple-element.72) | copy-start | bytes 3612676
  192.4 351.6 %reduce-scatter.8.cloned.1.call-start = ((), (), s32[]{:S(2)}) async-start(), calls=%async_computation.10 | async-start | bytes 1253376 | tf_op jit(solution)/shard_map/reduce_scatter | solution.py:503
  205.3 400.4 %reduce-scatter.12.cloned.1.call-start = ((), (), s32[]{:S(2)}) async-start(), calls=%async_computation.12 | async-start | bytes 1253376 | tf_op jit(solution)/shard_map/reduce_scatter | solution.py:503
  243.5 7.6 %copy-start.3 = (f32[4,8,384]{2,1,0:T(8,128)S(1)}, f32[4,8,384]{2,1,0:T(8,128)}, u32[]{:S(2)}) copy-start(f32[4,8,384]{2,1,0:T(8,128)} %get-tuple-element.54) | copy-start | bytes 147460
  243.5 7.6 %copy-start.5 = (f32[3,8,384]{2,1,0:T(8,128)S(1)}, f32[3,8,384]{2,1,0:T(8,128)}, u32[]{:S(2)}) copy-start(f32[3,8,384]{2,1,0:T(8,128)} %get-tuple-element.50) | copy-start | bytes 110596
  243.5 7.7 %copy-start.4 = (f32[8,1536]{1,0:T(8,128)S(1)}, f32[8,1536]{1,0:T(8,128)}, u32[]{:S(2)}) copy-start(f32[8,1536]{1,0:T(8,128)} %get-tuple-element.52) | copy-start | bytes 147460
  243.5 7.7 %copy-start.6 = (f32[8,768]{1,0:T(8,128)S(1)}, f32[8,768]{1,0:T(8,128)}, u32[]{:S(2)}) copy-start(f32[8,768]{1,0:T(8,128)} %get-tuple-element.56) | copy-start | bytes 73732
Sparse Core Ops, SparseCore 0:
  9.6 25.4 all-gather.4
  36.6 22.7 all-gather.6
  62.4 57.3 all-gather.8
  171.6 33.5 reduce-scatter.5
  207.4 34.6 reduce-scatter.9
  247.6 119.5 all-reduce.3
  373.2 108.9 reduce-scatter.13
  486.8 57.1 reduce-scatter.7
  548.6 57.0 reduce-scatter.11
